TPU v7x, 32 devices: a whole 2x2x4 slice. The times are simulated.
32 devices in a mesh: dp: 16 (over z, y, core), rep: 2 (over x).
Axes of the slice: x: 2, y: 2, z: 4, core: 2. Of those that a mesh axis runs over, the one named last changes fastest.
Arguments:
- images: bfloat16 [512, 7, 7, 2048], P(('dp', 'rep')), may hold values from -6 to 6
- labels: int32 [512], P(('dp', 'rep')), may hold values from 0 to 999
- conv1: float32 [2048, 512], P('rep'), may hold values from -0.125 to 0.125
- conv2: float32 [4608, 512], P('rep'), may hold values from -0.09375 to 0.09375
- classifier: float32 [512, 1000], P('rep'), may hold values from -0.9 to 0.9
- class_bias: float32 [1000], replicated, may hold values from -3 to 3
- batchnorm_parameters: float32 [2, 2, 512], replicated, may hold values from 0.25 to 1.75
- conv1_mom: float32 [2048, 512], P('rep'), may hold values from -0.0024414062 to 0.0024414062
- conv2_mom: float32 [4608, 512], P('rep'), may hold values from -0.0024414062 to 0.0024414062
- class_m: float32 [512, 1000], P('rep'), may hold values from -0.00061035156 to 0.00061035156
- class_v: float32 [512, 1000], P('rep'), may hold values from 7.8125e-10 to 3.125e-09
- bias_m: float32 [1000], replicated, may hold values from -0.0008544922 to 0.0008544922
- bias_v: float32 [1000], replicated, may hold values from 1.7578125e-09 to 7.03125e-09
- norm_m: float32 [2, 2, 512], replicated, may hold values from -0.00030517578 to 0.00030517578
- norm_v: float32 [2, 2, 512], replicated, may hold values from 1.953125e-10 to 7.8125e-10
- conv1_live: int32 [2048, 512], P('rep'), may hold values 0 or 1
- conv2_live: int32 [4608, 512], P('rep'), may hold values 0 or 1
- conv1_next: int32 [2048, 512], P('rep'), may hold values 0 or 1
- conv2_next: int32 [4608, 512], P('rep'), may hold values 0 or 1
Outputs:
- loss_sum: float32 [], replicated
- conv1_new: float32 [2048, 512], P('rep')
- conv2_new: float32 [4608, 512], P('rep')
- classifier_new: float32 [512, 1000], P('rep')
- class_bias_new: float32 [1000], replicated
- norm_new: float32 [2, 2, 512], replicated
- conv1_mom_new: float32 [2048, 512], P('rep')
- conv2_mom_new: float32 [4608, 512], P('rep')
- class_m_new: float32 [512, 1000], P('rep')
- class_v_new: float32 [512, 1000], P('rep')
- bias_m_new: float32 [1000], replicated
- bias_v_new: float32 [1000], replicated
- norm_m_new: float32 [2, 2, 512], replicated
- norm_v_first: float32 [2, 512], replicated
- norm_v_second: float32 [2, 512], replicated
All inputs are finite; a program needn't handle non-finite values. No bound on the sum of `conv1_live` or of `conv2_live` or of `conv1_next` or of `conv2_next` on one device may be relied on, other than what follows from the above.
Results may differ from a plain program's by a relative error of at most 0.0055.
The roundings to bfloat16 on the way count: a program that leaves them out, or rounds other values in their place, can miss the bound.
Values may be sent and summed in bfloat16 or wider, within the bound.
A program may use at most 256 MiB of HBM per device.

v0:
```python
import jax
import jax.numpy as jnp
from jax import lax
from jax.sharding import PartitionSpec as P

SIDE = 7
TURNS = 5
STEP = 5


HIGH = lax.Precision.HIGHEST
NORM_EPS = 1e-05
COEF_A = 3.4445
COEF_B = -4.775
COEF_C = 2.0315


def patches_of(act):
    count = act.shape[0]
    chans = act.shape[3]
    padded = jnp.pad(act, ((0, 0), (1, 1), (1, 1), (0, 0)))
    pieces = [padded[:, dy : dy + SIDE, dx : dx + SIDE, :] for dy in range(3) for dx in range(3)]
    return jnp.concatenate(pieces, axis=3).reshape(count * SIDE * SIDE, 9 * chans)


def fold_patches(grad_rows, count, chans):
    pieces = grad_rows.reshape(count, SIDE, SIDE, 9, chans)
    padded = jnp.zeros((count, SIDE + 2, SIDE + 2, chans), jnp.float32)
    for dy in range(3):
        for dx in range(3):
            padded = padded.at[:, dy : dy + SIDE, dx : dx + SIDE, :].add(
                pieces[:, :, :, 3 * dy + dx, :]
            )
    return padded[:, 1 : SIDE + 1, 1 : SIDE + 1, :].reshape(count * SIDE * SIDE, chans)


def across_rows(left, right):
    return lax.dot_general(
        left, right, (((0,), (0,)), ((), ())), preferred_element_type=jnp.float32
    )


def against_cols(left, right):
    return lax.dot_general(
        left, right, (((1,), (1,)), ((), ())), preferred_element_type=jnp.float32
    )


def batchnorm_forward(hidden, norm_gain, norm_shift, element_count):
    sums, squares = lax.psum(
        (jnp.sum(hidden, axis=0), jnp.sum(hidden * hidden, axis=0)), ("dp", "rep")
    )
    channel_mean = sums / element_count
    inverse_deviation = lax.rsqrt(squares / element_count - channel_mean * channel_mean + NORM_EPS)
    standardized = (hidden - channel_mean) * inverse_deviation
    return (norm_gain * standardized + norm_shift, standardized, inverse_deviation)


def batchnorm_backward(
    activation_gradient, normed_output, standardized, inverse_deviation, norm_gain, element_count
):
    sig = jax.nn.sigmoid(normed_output)
    normed_gradient = activation_gradient * sig * (1.0 + normed_output * (1.0 - sig))
    shift_gradient, gain_gradient = lax.psum(
        (jnp.sum(normed_gradient, axis=0), jnp.sum(normed_gradient * standardized, axis=0)),
        ("dp", "rep"),
    )
    hidden_gradient = (
        norm_gain
        * inverse_deviation
        * (
            normed_gradient
            - shift_gradient / element_count
            - standardized * gain_gradient / element_count
        )
    )
    return (hidden_gradient, gain_gradient, shift_gradient)


def gram_of(x):
    return lax.dot_general(x, x, (((0,), (0,)), ((), ())), precision=HIGH)


def newton_schulz(pair, summed):
    first, second = pair
    for turn in range(TURNS):
        gram_one, gram_two = summed(first, second)
        if turn == 0:
            scale_one = jnp.sqrt(jnp.trace(gram_one)) + 1e-07
            scale_two = jnp.sqrt(jnp.trace(gram_two)) + 1e-07
            first = first / scale_one
            second = second / scale_two
            gram_one = gram_one / (scale_one * scale_one)
            gram_two = gram_two / (scale_two * scale_two)
        inner_one = COEF_B * gram_one + COEF_C * jnp.dot(gram_one, gram_one, precision=HIGH)
        inner_two = COEF_B * gram_two + COEF_C * jnp.dot(gram_two, gram_two, precision=HIGH)
        first = COEF_A * first + jnp.dot(first, inner_one, precision=HIGH)
        second = COEF_A * second + jnp.dot(second, inner_two, precision=HIGH)
    return (first, second)


def adam_update(weight, first, second, grad, rate):
    first = 0.9 * first + 0.1 * grad
    second = 0.999 * second + 0.001 * grad * grad
    mhat = first / (1.0 - 0.9**STEP)
    vhat = second / (1.0 - 0.999**STEP)
    return (weight - rate * (mhat / (jnp.sqrt(vhat) + 1e-08) + 0.01 * weight), first, second)


def local(
    images,
    labels,
    conv1,
    conv2,
    classifier,
    class_bias,
    batchnorm_parameters,
    conv1_mom,
    conv2_mom,
    class_m,
    class_v,
    bias_m,
    bias_v,
    norm_m,
    norm_v,
    conv1_live,
    conv2_live,
    conv1_next,
    conv2_next,
):
    count = images.shape[0]
    c_in = images.shape[3]
    c_mid = conv1.shape[1]
    classes = class_bias.shape[0]
    all_images = count * lax.axis_size("dp") * lax.axis_size("rep")
    element_count = all_images * SIDE * SIDE
    part_one = (conv1 * conv1_live.astype(jnp.float32)).astype(jnp.bfloat16)
    part_two = (conv2 * conv2_live.astype(jnp.float32)).astype(jnp.bfloat16)
    part_head = classifier.astype(jnp.bfloat16)
    w1b, w2b, wcb = (
        lax.all_gather(part_one, "rep", axis=0, tiled=True),
        lax.all_gather(part_two, "rep", axis=0, tiled=True),
        lax.all_gather(part_head, "rep", axis=0, tiled=True),
    )
    inputs = images.reshape(count * SIDE * SIDE, c_in)
    hidden_first = jnp.dot(inputs, w1b, preferred_element_type=jnp.float32)
    normed_first, standardized_first, inverse_deviation_first = batchnorm_forward(
        hidden_first, batchnorm_parameters[0, 0], batchnorm_parameters[0, 1], element_count
    )
    a1 = jax.nn.silu(normed_first).astype(jnp.bfloat16)
    patches = patches_of(a1.reshape(count, SIDE, SIDE, c_mid))
    hidden_second = jnp.dot(patches, w2b, preferred_element_type=jnp.float32)
    normed_second, standardized_second, inverse_deviation_second = batchnorm_forward(
        hidden_second, batchnorm_parameters[1, 0], batchnorm_parameters[1, 1], element_count
    )
    a2 = jax.nn.silu(normed_second)
    pooled = jnp.mean(a2.reshape(count, SIDE * SIDE, c_mid), axis=1).astype(jnp.bfloat16)
    logits = jnp.dot(pooled, wcb, preferred_element_type=jnp.float32) + class_bias
    lse = jax.nn.logsumexp(logits, axis=1)
    onehot = (labels[:, None] == jnp.arange(classes, dtype=jnp.int32)[None, :]).astype(jnp.float32)
    target = jnp.sum(logits * onehot, axis=1)
    probs = jnp.exp(logits - lse[:, None])
    grad_logits = (probs - onehot) / all_images
    loss_sum, g_bias = lax.psum(
        (jnp.sum(lse - target), jnp.sum(grad_logits, axis=0)), ("dp", "rep")
    )
    grad_z = grad_logits.astype(jnp.bfloat16)
    g_class = across_rows(pooled, grad_z)
    grad_pooled = against_cols(grad_z, wcb) / (SIDE * SIDE)
    gradient_activation_second = jnp.broadcast_to(
        grad_pooled[:, None, :], (count, SIDE * SIDE, c_mid)
    ).reshape(-1, c_mid)
    grad_h2, gain_two, shift_two = batchnorm_backward(
        gradient_activation_second,
        normed_second,
        standardized_second,
        inverse_deviation_second,
        batchnorm_parameters[1, 0],
        element_count,
    )
    grad_h2 = grad_h2.astype(jnp.bfloat16)
    g_conv2 = across_rows(patches, grad_h2)
    gradient_activation_first = fold_patches(against_cols(grad_h2, w2b), count, c_mid)
    grad_h1, gain_one, shift_one = batchnorm_backward(
        gradient_activation_first,
        normed_first,
        standardized_first,
        inverse_deviation_first,
        batchnorm_parameters[0, 0],
        element_count,
    )
    g_conv1 = across_rows(inputs, grad_h1.astype(jnp.bfloat16))
    rows_one, rows_two, rows_head = (
        lax.psum_scatter(g_conv1, "rep", scatter_dimension=0, tiled=True),
        lax.psum_scatter(g_conv2, "rep", scatter_dimension=0, tiled=True),
        lax.psum_scatter(g_class, "rep", scatter_dimension=0, tiled=True),
    )
    rows_one, rows_two, rows_head = lax.psum((rows_one, rows_two, rows_head), "dp")
    mom_one = 0.5 * conv1_mom + rows_one
    mom_two = 0.5 * conv2_mom + rows_two

    def summed(first, second):
        return lax.psum((gram_of(first), gram_of(second)), "rep")

    ortho_one, ortho_two = newton_schulz((mom_one, mom_two), summed)
    conv1_new = (conv1 - 1.0 * ortho_one) * conv1_next.astype(jnp.float32)
    conv2_new = (conv2 - 1.0 * ortho_two) * conv2_next.astype(jnp.float32)
    head_new, head_m, head_v = adam_update(classifier, class_m, class_v, rows_head, 0.03)
    bias_new, first_b, second_b = adam_update(class_bias, bias_m, bias_v, g_bias, 0.2)
    g_norm = jnp.stack([jnp.stack([gain_one, shift_one]), jnp.stack([gain_two, shift_two])])
    norm_new, first_n, second_n = adam_update(batchnorm_parameters, norm_m, norm_v, g_norm, 0.2)
    return (
        loss_sum,
        conv1_new,
        conv2_new,
        head_new,
        bias_new,
        norm_new,
        mom_one,
        mom_two,
        head_m,
        head_v,
        first_b,
        second_b,
        first_n,
        second_n[0],
        second_n[1],
    )


def solution(mesh):
    placed = (
        P(("dp", "rep"), None, None, None),
        P(("dp", "rep")),
        P("rep", None),
        P("rep", None),
        P("rep", None),
        P(),
        P(),
        P("rep", None),
        P("rep", None),
        P("rep", None),
        P("rep", None),
        P(),
        P(),
        P(),
        P(),
        P("rep", None),
        P("rep", None),
        P("rep", None),
        P("rep", None),
    )
    return jax.shard_map(
        local,
        mesh=mesh,
        in_specs=placed,
        out_specs=(
            P(),
            P("rep", None),
            P("rep", None),
            P("rep", None),
            P(),
            P(),
            P("rep", None),
            P("rep", None),
            P("rep", None),
            P("rep", None),
            P(),
            P(),
            P(),
            P(),
            P(),
        ),
        check_vma=False,
    )
```

profile of v0, /device:TPU:0, one launch (start us, length us, event | category | flops | bytes accessed | tf_op | source)
XLA Modules:
  0.0 1235.5 jit_solution(8415492735545407372)
XLA Ops:
  7.2 3.7 multiply_convert_fusion.1
  11.0 6.6 multiply_convert_fusion
  17.7 3.6 copy.260
  21.3 5.7 reshape.464
  29.7 26.8 %all_gather.11 = bf16[512,1000]{0,1:T(8,128)(2,1)S(1)} all-gather(bf16[256,1000]{0,1:T(8,128)(2,1)S(1)} %convert_element_type.47), channel_id=1, replica_groups=mesh['dp'=16,'rep'=2] {'rep'}, dimensions={0}, use_global_device_ids=true | all-gather | bytes 1536000 | tf_op jit(solution)/shard_map/all_gather | solution.py:143
  57.9 4.4 fusion.58
  62.3 40.1 %all-reduce.5 = (f32[512]{0:T(512)S(1)}, f32[512]{0:T(512)S(1)}) all-reduce(f32[512]{0:T(512)S(1)} %get-tuple-element.295, f32[512]{0:T(512)S(1)} %get-tuple-element.294), channel_id=1, replica_groups=mesh['dp'=16,'rep'=2] {'dp','rep'}, use_global_device_ids=true, to_apply=%region_3.0 | all-reduce | flops 1024 | bytes 8192 | tf_op jit(solution)/shard_map/psum | solution.py:50
  104.7 7.0 pad_slice_fusion
  124.5 2.2 concatenate.52
  128.0 2.2 constant_dynamic-update-slice_fusion.8
  139.8 7.6 fusion.57
  147.4 41.0 %all-reduce.4 = (f32[512]{0:T(512)S(1)}, f32[512]{0:T(512)S(1)}) all-reduce(f32[512]{0:T(512)S(1)} %get-tuple-element.293, f32[512]{0:T(512)S(1)} %get-tuple-element.292), channel_id=1, replica_groups=mesh['dp'=16,'rep'=2] {'dp','rep'}, use_global_device_ids=true, to_apply=%region_7.8 | all-reduce | flops 1024 | bytes 8192 | tf_op jit(solution)/shard_map/psum | solution.py:50
  190.7 2.9 reshape.466
  199.9 2.3 fusion.56
  202.2 39.6 %all-reduce.3 = (f32[512]{0:T(512)S(1)}, f32[512]{0:T(512)S(1)}) all-reduce(f32[512]{0:T(512)S(1)} %get-tuple-element.291, f32[512]{0:T(512)S(1)} %get-tuple-element.290), channel_id=1, replica_groups=mesh['dp'=16,'rep'=2] {'dp','rep'}, use_global_device_ids=true, to_apply=%region_17.18 | all-reduce | flops 1024 | bytes 8192 | tf_op jit(solution)/shard_map/psum | solution.py:64
  243.1 9.5 fusion.67
  252.6 18.2 %reshape.468 = f32[16,7,7,9,512]{4,3,2,1,0:T(8,128)} reshape(f32[784,4608]{1,0:T(8,128)} %fusion.67) | data formatting | bytes 28901376 | tf_op jit(solution)/shard_map/reshape | solution.py:27
  270.8 44.5 %fusion.62 = (f32[16,7,7,1,512]{4,3,2,1,0:T(1,128)}, f32[16,7,7,1,512]{4,3,2,1,0:T(1,128)}, f32[16,7,7,1,512]{4,3,2,1,0:T(1,128)}, f32[16,7,7,1,512]{4,3,2,1,0:T...) fusion(f32[16,7,7,9,512]{4,3,2,1,0:T(8,128)} %reshape.468), kind=kLoop, calls=%fused_computation.157 | loop fusion | bytes 28901376 | tf_op jit(solution)/shard_map/slice | solution.py:32
  315.9 3.3 fusion.12
  319.2 2.4 fusion.5
  332.9 2.3 fusion.55
  335.1 41.5 %all-reduce.2 = (f32[]{:T(128)}, f32[512]{0:T(512)S(1)}, f32[512]{0:T(512)S(1)}, f32[1000]{0:T(1024)S(1)}) all-reduce(f32[]{:T(128)} %subtract_reduce_fusion, f32[512]{0:T(512)S(1)} %get-tuple-element.289, f32[512]{0:T(512)S(1)} %get-tuple-element.288, f32[1000]{0:T(1024)S(1)} %get-tuple-element.296), channel_id=1, replica_groups=mesh['dp'=16,'rep'=2] {'dp','rep'}, use_global_device_ids=true, to_apply=%region_13.14 | all-reduce | flops 2025 | bytes 16200 | tf_op jit(solution)/shard_map/psum | solution.py:164
  376.6 6.4 convolution_bitcast_fusion
  384.2 10.8 fusion.73
  395.0 42.3 %reduce-scatter.4.cloned.1.call-done = f32[1024,512]{0,1:T(8,128)} async-done(((f32[2048,512]{0,1:T(8,128)}), f32[1024,512]{0,1:T(8,128)}) %reduce-scatter.4.cloned.1.call-update) | async-done | bytes 2097168 | tf_op jit(solution)/shard_map/reduce_scatter | solution.py:194
  437.4 112.8 %reduce-scatter.6.cloned.1.call-done = f32[2304,512]{1,0:T(8,128)} async-done(((f32[4608,512]{1,0:T(8,128)}), f32[2304,512]{1,0:T(8,128)}) %reduce-scatter.6.cloned.1.call-update) | async-done | bytes 4718608 | tf_op jit(solution)/shard_map/reduce_scatter | solution.py:195
  553.8 163.2 %all-reduce.19.cloned.1.call-done = (f32[1024,512]{0,1:T(8,128)}, f32[2304,512]{1,0:T(8,128)}, f32[256,1000]{0,1:T(8,128)}) async-done(((f32[1024,512]{0,1:T(8,128)}, f32[2304,512]{1,0:T(8,128)}, f32[256,1000]{0,1:T(8,128)}), (f32[1024,512]{0,1:T(8,128)}, f32[2304,512]{1,0:T(8,128)}, f32[256,1000]{0,1:T(8,128)})) %all-reduce.19.cloned.1.call-update) | async-done | bytes 7839760 | tf_op jit(solution)/shard_map/psum | solution.py:198
  717.0 4.9 multiply_add_fusion
  722.0 8.9 fusion.74
  731.3 4.9 fusion.68
  736.3 63.2 %all-reduce.29.cloned.1.call-done = (f32[512,512]{1,0:T(8,128)}, f32[512,512]{1,0:T(8,128)}) async-done(((f32[512,512]{1,0:T(8,128)}, f32[512,512]{1,0:T(8,128)}), (f32[512,512]{1,0:T(8,128)}, f32[512,512]{1,0:T(8,128)})) %all-reduce.29.cloned.1.call-update) | async-done | bytes 2097168 | tf_op jit(solution)/shard_map/psum | solution.py:203
  799.4 2.3 select_reduce_fusion
  802.4 4.0 fusion.24
  806.4 7.8 convolution_add_fusion.4
  814.2 8.8 fusion.75
  823.7 4.0 fusion.29
  827.7 3.7 multiply_add_fusion.4
  832.7 4.7 fusion.69
  837.5 63.2 %all-reduce.27.cloned.1.call-done = (f32[512,512]{1,0:T(8,128)}, f32[512,512]{1,0:T(8,128)}) async-done(((f32[512,512]{1,0:T(8,128)}, f32[512,512]{1,0:T(8,128)}), (f32[512,512]{1,0:T(8,128)}, f32[512,512]{1,0:T(8,128)})) %all-reduce.27.cloned.1.call-update) | async-done | bytes 2097168 | tf_op jit(solution)/shard_map/psum | solution.py:203
  900.7 3.9 fusion.23
  904.6 11.9 convolution_add_fusion.3
  916.6 8.6 fusion.76
  927.1 3.9 multiply_add_fusion.3
  932.4 4.5 fusion.70
  937.0 63.2 %all-reduce.25.cloned.1.call-done = (f32[512,512]{1,0:T(8,128)}, f32[512,512]{1,0:T(8,128)}) async-done(((f32[512,512]{1,0:T(8,128)}, f32[512,512]{1,0:T(8,128)}), (f32[512,512]{1,0:T(8,128)}, f32[512,512]{1,0:T(8,128)})) %all-reduce.25.cloned.1.call-update) | async-done | bytes 2097168 | tf_op jit(solution)/shard_map/psum | solution.py:203
  1000.2 3.9 fusion.22
  1004.1 11.7 convolution_add_fusion.2
  1015.8 8.6 fusion.77
  1026.4 4.1 multiply_add_fusion.2
  1031.8 4.5 fusion.71
  1036.4 63.2 %all-reduce.23.cloned.1.call-done = (f32[512,512]{1,0:T(8,128)}, f32[512,512]{1,0:T(8,128)}) async-done(((f32[512,512]{1,0:T(8,128)}, f32[512,512]{1,0:T(8,128)}), (f32[512,512]{1,0:T(8,128)}, f32[512,512]{1,0:T(8,128)})) %all-reduce.23.cloned.1.call-update) | async-done | bytes 2097168 | tf_op jit(solution)/shard_map/psum | solution.py:203
  1099.6 3.9 fusion.21
  1103.6 11.7 convolution_add_fusion.1
  1115.3 8.6 fusion.78
  1125.8 4.0 multiply_add_fusion.1
  1131.2 4.5 fusion.72
  1135.7 2.9 copy.277
  1138.6 2.9 copy.278
  1145.3 4.2 multiply_subtract_fusion
  1149.5 49.4 %all-reduce.21.cloned.1.call-done = (f32[512,512]{1,0:T(8,128)}, f32[512,512]{1,0:T(8,128)}) async-done(((f32[512,512]{1,0:T(8,128)}, f32[512,512]{1,0:T(8,128)}), (f32[512,512]{1,0:T(8,128)}, f32[512,512]{1,0:T(8,128)})) %all-reduce.21.cloned.1.call-update) | async-done | bytes 2097168 | tf_op jit(solution)/shard_map/psum | solution.py:203
  1198.9 3.9 fusion.20
  1202.8 4.1 fusion.25
  1207.0 4.0 convert_multiply_fusion
  1212.8 15.7 %fusion.1 = f32[2304,512]{1,0:T(8,128)} fusion(f32[2304,512]{1,0:T(8,128)} %param.40, f32[2304,512]{1,0:T(8,128)} %copy-done, f32[512,512]{1,0:T(8,128)S(1)} %fusion.20, s32[2304,512]{1,0:T(8,128)} %param.55), kind=kOutput, calls=%fused_computation.14 | convolution fusion | flops 7253655552 | bytes 19922944 | tf_op jit(solution)/shard_map/dot_general | solution.py:98
  (226 shorter events, 73.7 us)
Async XLA Ops:
  7.2 50.7 %all-gather.3.cloned.1.call-start = ((), (), s32[]{:S(2)}) async-start(), calls=%async_computation.3 | async-start | bytes 3145728 | tf_op jit(solution)/shard_map/all_gather | solution.py:141
  11.0 128.8 %all-gather.5.cloned.1.call-start = ((), (), s32[]{:S(2)}) async-start(), calls=%async_computation.4 | async-start | bytes 7077888 | tf_op jit(solution)/shard_map/all_gather | solution.py:142
  11.0 6.7 copy-start.35
  17.7 377.4 %reduce-scatter.8.cloned.1.call-start = ((), (), s32[]{:S(2)}) async-start(), calls=%async_computation.7 | async-start | bytes 3072000 | tf_op jit(solution)/shard_map/reduce_scatter | solution.py:196
  21.3 5.8 copy-start.28
  21.3 7.0 copy-start.65
  21.3 7.7 copy-start.50
  29.6 73.3 %copy-start.41 = (f32[1,1,512]{2,1,0:T(1,128)}, f32[1,1,512]{2,1,0:T(1,128)S(1)}, u32[]{:S(2)}) copy-start(f32[1,1,512]{2,1,0:T(1,128)S(1)} %get-tuple-element.353) | copy-start | bytes 6148
  29.7 73.3 %copy-start.45 = (f32[1,1,512]{2,1,0:T(1,128)}, f32[1,1,512]{2,1,0:T(1,128)S(1)}, u32[]{:S(2)}) copy-start(f32[1,1,512]{2,1,0:T(1,128)S(1)} %get-tuple-element.352) | copy-start | bytes 6148
  62.3 72.1 %copy-start.11 = (f32[512,784]{0,1:T(8,128)}, f32[512,784]{0,1:T(8,128)S(1)}, u32[]{:S(2)}) copy-start(f32[512,784]{0,1:T(8,128)S(1)} %get-tuple-element.365) | copy-start | bytes 4816900
  128.0 4.4 copy-start.34
  128.0 5.4 copy-start.33
  130.2 4.2 copy-start.42
  130.2 4.2 copy-start.46
  133.4 2.4 copy-start.32
  134.4 2.4 copy-start.31
  135.9 2.0 copy-start.29
  135.9 3.0 copy-start.30
  139.8 48.6 %copy-start.48 = (f32[1,1,512]{2,1,0:T(1,128)S(1)}, f32[1,1,512]{2,1,0:T(1,128)}, u32[]{:S(2)}) copy-start(f32[1,1,512]{2,1,0:T(1,128)} %get-tuple-element.351) | copy-start | bytes 6148
  139.8 49.2 %copy-start.52 = (f32[1,1,512]{2,1,0:T(1,128)S(1)}, f32[1,1,512]{2,1,0:T(1,128)}, u32[]{:S(2)}) copy-start(f32[1,1,512]{2,1,0:T(1,128)} %get-tuple-element.354) | copy-start | bytes 6148
  189.0 1.6 copy-start.43
  190.7 4.6 copy-start.54
  193.5 2.5 copy-start.59
  196.0 2.2 copy-start.61
  199.9 41.9 %copy-start.56 = (f32[512]{0:T(512)S(1)}, f32[512]{0:T(512)}, u32[]{:S(2)}) copy-start(f32[512]{0:T(512)} %get-tuple-element.357) | copy-start | bytes 6148
  315.8 121.6 %reduce-scatter.4.cloned.1.call-start = ((), (), s32[]{:S(2)}) async-start(), calls=%async_computation.5 | async-start | bytes 6291456 | tf_op jit(solution)/shard_map/reduce_scatter | solution.py:194
  315.9 3.3 copy-start.24
  319.1 2.4 copy-start.23
  321.5 1.8 copy-start.22
  330.6 2.2 copy-start.12
  330.6 2.2 copy-start.47
  332.9 43.8 %copy-start.40 = (f32[512]{0:T(512)S(1)}, f32[512]{0:T(512)}, u32[]{:S(2)}) copy-start(f32[512]{0:T(512)} %get-tuple-element.355) | copy-start | bytes 6148
  383.1 167.1 %reduce-scatter.6.cloned.1.call-start = ((), (), s32[]{:S(2)}) async-start(), calls=%async_computation.6 | async-start | bytes 14155776 | tf_op jit(solution)/shard_map/reduce_scatter | solution.py:195
  395.0 322.0 %all-reduce.19.cloned.1.call-start = ((), (), s32[]{:S(2)}) async-start(), calls=%async_computation.8 | async-start | bytes 15679488 | tf_op jit(solution)/shard_map/psum | solution.py:198
  550.2 1.6 copy-start.37
  550.2 249.2 %all-reduce.29.cloned.1.call-start = ((), (), s32[]{:S(2)}) async-start(), calls=%async_computation.13 | async-start | bytes 4194304 | tf_op jit(solution)/shard_map/psum | solution.py:203
  721.9 8.9 copy-start.3
  722.0 8.9 copy-start.15
  722.0 8.9 copy-start.36
  736.2 164.5 %all-reduce.27.cloned.1.call-start = ((), (), s32[]{:S(2)}) async-start(), calls=%async_computation.12 | async-start | bytes 4194304 | tf_op jit(solution)/shard_map/psum | solution.py:203
  799.4 7.0 slice-start
  802.4 4.0 slice-start.1
  814.2 8.8 copy-start.4
  837.5 162.7 %all-reduce.25.cloned.1.call-start = ((), (), s32[]{:S(2)}) async-start(), calls=%async_computation.11 | async-start | bytes 4194304 | tf_op jit(solution)/shard_map/psum | solution.py:203
  916.6 8.6 copy-start.1
  916.6 8.6 copy-start.25
  925.2 1.9 copy-start.14
  936.9 162.7 %all-reduce.23.cloned.1.call-start = ((), (), s32[]{:S(2)}) async-start(), calls=%async_computation.10 | async-start | bytes 4194304 | tf_op jit(solution)/shard_map/psum | solution.py:203
  1015.8 8.6 copy-start.2
  1015.8 8.6 copy-start.26
  1024.4 1.9 copy-start.6
  1036.4 162.6 %all-reduce.21.cloned.1.call-start = ((), (), s32[]{:S(2)}) async-start(), calls=%async_computation.9 | async-start | bytes 4194304 | tf_op jit(solution)/shard_map/psum | solution.py:203
  1115.2 8.7 copy-start
  1115.3 8.7 copy-start.27
  1123.9 1.9 copy-start.8
  1138.6 3.0 copy-start.51
  1138.6 3.0 copy-start.57
  1138.6 3.0 copy-start.58
  1138.6 4.3 copy-start.55
  1138.6 4.3 copy-start.63
  1138.6 4.3 copy-start.64
  1198.9 8.1 copy-start.16
  1198.9 8.1 copy-start.17
  1202.8 4.2 copy-start.10
  (15 other events, 20.2 us)
Sparse Core Ops, SparseCore 0:
  11.1 46.7 all-gather.2
  59.5 63.6 all-gather.4
  315.9 32.5 reduce-scatter.7
  383.2 54.1 reduce-scatter.3
  439.6 110.5 reduce-scatter.5
  554.6 162.3 all-reduce.18
  736.3 63.0 all-reduce.28
  837.6 63.0 all-reduce.26
  937.0 63.0 all-reduce.24
  1036.5 63.0 all-reduce.22
  1135.8 63.0 all-reduce.20
where the time goes:
time: 1240 us
  waiting for transfers between devices  622 us (50%)
  matrix products  220 us (18%)
  blocking collectives  189 us (15%)
  local copies, waits for them, and re-layouts  142 us (11%)
  other arithmetic  45.3 us (4%)
  between operations  16.5 us (1%)
    psum x5, waiting for transfers between devices, summed(): return lax.psum((gram_of(first), gram_of(second)), 'rep')  302 us
    psum x1, waiting for transfers between devices, local(): lax.psum((rows_one, rows_two, rows_head), 'dp')  163 us
    reduce_scatter x1, waiting for transfers between devices, local(): lax.psum_scatter(g_conv2, 'rep', scatter_dimension=0, tiled=True)  113 us
    psum x2, blocking collectives, batchnorm_forward(): lax.psum((jnp.sum(hidden, axis=0), jnp.sum(hidden * hidden, axis=0)), ('d...  81.1 us
    dot_general x10, matrix products, gram_of(): return lax.dot_general(x, x, (((0,), (0,)), ((), ())), precision=HIGH)  66.7 us
    dot_general x5, matrix products, newton_schulz(): second = COEF_A * second + jnp.dot(second, inner_two, precision=HIGH)  58.8 us
    slice x2, local copies, waits for them, and re-layouts, fold_patches(): pieces[:, :, :, 3 * dy + dx, :]  44.7 us
    reduce_scatter x1, waiting for transfers between devices, local(): lax.psum_scatter(g_conv1, 'rep', scatter_dimension=0, tiled=True)  42.3 us
  transfers between devices with their start and end apart: 11, of which 9 were waited for; matrix products, arithmetic and copies ran while one was open for 9% of the time, Pallas kernels for 0%

commit v1 on v0

--- a/solution.py
+++ b/solution.py
@@ -1,11 +1,380 @@
+import functools
+
 import jax
 import jax.numpy as jnp
 from jax import lax
+from jax.experimental import pallas as pl
+from jax.experimental.pallas import tpu as pltpu
 from jax.sharding import PartitionSpec as P
 
 SIDE = 7
 TURNS = 5
 STEP = 5
+NORM_EPS = 1e-05
+COEF_A = 3.4445
+COEF_B = -4.775
+COEF_C = 2.0315
+MESH = pl.DeviceIdType.MESH
+BF = jnp.bfloat16
+F32 = jnp.float32
+DMA = pltpu.SemaphoreType.DMA
+
+
+def nn(a, b):
+    return jnp.dot(a, b, preferred_element_type=F32)
+
+
+def nt(a, b):
+    return lax.dot_general(a, b, (((1,), (1,)), ((), ())), preferred_element_type=F32)
+
+
+def tn(a, b):
+    return lax.dot_general(a, b, (((0,), (0,)), ((), ())), preferred_element_type=F32)
+
+
+def sigmoid(v):
+    return 1.0 / (1.0 + jnp.exp(-v))
+
+
+class Place:
+    def __init__(self, n_dp, n_rep):
+        self.n_dp, self.n_rep = n_dp, n_rep
+        self.chips = n_dp // 2 * n_rep
+        self.dp, self.rep = lax.axis_index("dp"), lax.axis_index("rep")
+        self.core = lax.rem(self.dp, 2)
+        self.chip = self.dp // 2 * n_rep + self.rep
+
+    def flip(self, bit):
+        half = 1 << bit
+        set_now = lax.rem(self.dp // half, 2)
+        return {"dp": self.dp + half - 2 * half * set_now, "rep": self.rep}
+
+    def other_chip(self, step):
+        to = lax.rem(self.chip + step, self.chips)
+        return {"dp": to // self.n_rep * 2 + self.core, "rep": lax.rem(to, self.n_rep)}
+
+    def other_rep(self, step):
+        return {"dp": self.dp, "rep": lax.rem(self.rep + step, self.n_rep)}
+
+
+def send(src, dst, send_sem, recv_sem, to):
+    copy = pltpu.make_async_remote_copy(src, dst, send_sem, recv_sem, to, MESH)
+    copy.start()
+
+
+def wait_bytes(ref, sem):
+    pltpu.make_async_copy(ref, ref, sem).wait()
+
+
+def enter(place):
+    barrier = pltpu.get_barrier_semaphore()
+
+    def greet(step, carry):
+        pl.semaphore_signal(barrier, 1, device_id=place.other_chip(step), device_id_type=MESH)
+        return carry
+
+    lax.fori_loop(1, place.chips, greet, 0)
+    pl.semaphore_signal(barrier, 1, device_id=place.flip(0), device_id_type=MESH)
+    pl.semaphore_wait(barrier, place.chips)
+
+
+def sum_over_all(place, value, pair_buf, chip_buf, sems, meanwhile=None):
+    pair_buf[place.core] = value
+    mine = pair_buf.at[place.core]
+    send(mine, mine, sems.at[0], sems.at[1], place.flip(0))
+    wait_bytes(mine, sems.at[1])
+    chip_buf[place.chip] = pair_buf[0] + pair_buf[1]
+    block = chip_buf.at[place.chip]
+
+    def one(step, carry):
+        send(block, block, sems.at[2], sems.at[3], place.other_chip(step))
+        return carry
+
+    lax.fori_loop(1, place.chips, one, 0)
+    if meanwhile is not None:
+        meanwhile()
+    wait_bytes(chip_buf.at[pl.ds(0, place.chips - 1)], sems.at[3])
+    total = jnp.sum(chip_buf[...], axis=0)
+    wait_bytes(mine, sems.at[0])
+    wait_bytes(chip_buf.at[pl.ds(0, place.chips - 1)], sems.at[2])
+    return total
+
+
+class Gather:
+    def __init__(self, place, buf, pieces, sems):
+        self.place, self.buf, self.pieces, self.sems = place, buf, pieces, sems
+        self.quarter = buf.shape[1] // 4
+        self.rows = self.quarter // pieces
+        self.y = lax.rem(place.dp // 2, 2)
+
+    def at(self, block, y, piece):
+        first = self.place.core * (2 * self.quarter) + y * self.quarter + piece * self.rows
+        return self.buf.at[block, pl.ds(pl.multiple_of(first, 16), self.rows)]
+
+    def blocks(self):
+        return [lax.rem(self.place.rep + step, self.place.n_rep) for step in range(1, self.place.n_rep)]
+
+    def size(self):
+        return self.buf.at[pl.ds(0, self.place.n_rep - 1), pl.ds(0, self.rows)]
+
+    def start(self, piece):
+        mine = self.at(self.place.rep, self.y, piece)
+        for step in range(1, self.place.n_rep):
+            send(mine, mine, self.sems.at[0, piece, 0], self.sems.at[0, piece, 1], self.place.other_rep(step))
+
+    def hop_y(self, piece):
+        wait_bytes(self.size(), self.sems.at[0, piece, 1])
+        for block in self.blocks():
+            here = self.at(block, self.y, piece)
+            send(here, here, self.sems.at[1, piece, 0], self.sems.at[1, piece, 1], self.place.flip(1))
+            send(here, here, self.sems.at[2, piece, 0], self.sems.at[2, piece, 1], self.place.flip(0))
+
+    def hop_core(self, piece):
+        wait_bytes(self.size(), self.sems.at[1, piece, 1])
+        for block in self.blocks():
+            here = self.at(block, 1 - self.y, piece)
+            send(here, here, self.sems.at[3, piece, 0], self.sems.at[3, piece, 1], self.place.flip(0))
+
+    def finish(self, piece):
+        wait_bytes(self.size(), self.sems.at[2, piece, 1])
+        wait_bytes(self.size(), self.sems.at[3, piece, 1])
+
+    def drain(self):
+        for piece in range(self.pieces):
+            for hop in range(4):
+                wait_bytes(self.size(), self.sems.at[hop, piece, 0])
+
+
+def norm_of(total, count):
+    mean = total[0:1] / count
+    return mean, lax.rsqrt(total[1:2] / count - mean * mean + NORM_EPS)
+
+
+def over_pixels(step, init, images):
+    def body(pixel, carry):
+        return step(pixel, pl.multiple_of(pixel * images, 16), carry)
+
+    return lax.fori_loop(0, SIDE * SIDE, body, init, unroll=7)
+
+
+def fold(acc):
+    return jnp.sum(acc, axis=0, keepdims=True)
+
+
+def sums_of(h_ref, images):
+    chans = h_ref.shape[1]
+
+    def step(pixel, row, carry):
+        v = h_ref[pl.ds(row, images), :]
+        return carry[0] + v, carry[1] + v * v
+
+    zero = jnp.zeros((images, chans), F32)
+    one, two = over_pixels(step, (zero, zero), images)
+    return jnp.concatenate([fold(one), fold(two)], axis=0)
+
+
+def put_padded(pad_ref, pixel, value, images):
+    y, x = pixel // SIDE, lax.rem(pixel, SIDE)
+    pad_ref[1 + y, pl.ds(pl.multiple_of((1 + x) * images, 16), images), :] = value
+
+
+def clear_border(pad_ref, images):
+    line = SIDE * images
+    pad_ref[0] = jnp.zeros(pad_ref.shape[1:], pad_ref.dtype)
+    pad_ref[SIDE + 1] = jnp.zeros(pad_ref.shape[1:], pad_ref.dtype)
+    edge = jnp.zeros((SIDE, images, pad_ref.shape[2]), pad_ref.dtype)
+    pad_ref[1 : SIDE + 1, 0:images, :] = edge
+    pad_ref[1 : SIDE + 1, images + line : 2 * images + line, :] = edge
+
+
+def build_patches(pad_ref, to_ref):
+    rows, chans = to_ref.shape[0], pad_ref.shape[2]
+    line = rows // SIDE
+    images = line // SIDE
+    for k in range(9):
+        dy, dx = divmod(k, 3)
+        piece = pad_ref[dy : dy + SIDE, dx * images : dx * images + line, :]
+        to_ref[:, k * chans : (k + 1) * chans] = piece.reshape(rows, chans)
+
+
+def kernel_a(n_dp, n_rep, *refs):
+    (x_hbm, w1_hbm, w2_hbm, head_hbm, live1_hbm, live2_hbm, bias_ref, norm_ref, label_ref,
+     h1_ref, h2_ref, pad_ref, w2b, stat_ref, dz_ref, pooled_ref, loss_ref, gbias_ref, dpool_ref,
+     x_ref, f1, i1, f2, i2, fh, w1b, head_b, patches, bias_pad, pair_buf, chip_buf,
+     load_sem, w1_sem, w2_sem, head_sem, sum_sem) = refs
+    place = Place(n_dp, n_rep)
+    core, rep = place.core, place.rep
+    half1, half2, mid = w1b.shape[1], w2b.shape[1], w1b.shape[2]
+    classes, head_cols = fh.shape
+    wide = head_b.shape[1]
+    rows = x_ref.shape[0]
+    images = rows // (SIDE * SIDE)
+    all_images = images * n_dp * n_rep
+    count = all_images * SIDE * SIDE
+
+    pairs = [(w1_hbm, f1), (live1_hbm, i1), (w2_hbm, f2), (live2_hbm, i2), (x_hbm, x_ref), (head_hbm, fh)]
+    loads = [pltpu.make_async_copy(a, b, load_sem.at[k]) for k, (a, b) in enumerate(pairs)]
+    for load in loads:
+        load.start()
+    g1, g2, gh = Gather(place, w1b, 2, w1_sem), Gather(place, w2b, 3, w2_sem), Gather(place, head_b, 1, head_sem)
+
+    def mask(value, live, to, first, size):
+        at = pl.ds(pl.multiple_of(first, 16), size)
+        to[rep, at, :] = (value[at, :] * live[at, :].astype(F32)).astype(BF)
+
+    def spread(gather, value, live, to):
+        quarter = gather.quarter
+        mine = core * 2 + gather.y
+        for piece in range(gather.pieces):
+            mask(value, live, to, mine * quarter + piece * gather.rows, gather.rows)
+            gather.start(piece)
+        for other in range(1, 4):
+            mask(value, live, to, lax.rem(mine + other, 4) * quarter, quarter)
+
+    loads[0].wait()
+    loads[1].wait()
+    enter(place)
+    spread(g1, f1, i1, w1b)
+    loads[2].wait()
+    loads[3].wait()
+    spread(g2, f2, i2, w2b)
+    loads[5].wait()
+    head_b[rep, 0:classes, :] = fh[...].astype(BF)
+    head_b[rep, classes:, :] = jnp.zeros((wide - classes, head_cols), BF)
+    gh.start(0)
+    clear_border(pad_ref, images)
+    bias_pad[:, 0:classes] = bias_ref[...]
+    bias_pad[:, classes:] = jnp.zeros((1, wide - classes), F32)
+    loads[4].wait()
+
+    def cols(block, half):
+        return pl.ds(pl.multiple_of(block * half, 128), half)
+
+    h1_ref[...] = nn(x_ref[:, cols(rep, half1)], w1b[rep])
+    for piece in range(2):
+        g1.hop_y(piece)
+    for piece in range(2):
+        g1.hop_core(piece)
+    g2.hop_y(0)
+    for piece in range(2):
+        g1.finish(piece)
+    for block in g1.blocks():
+        h1_ref[...] += nn(x_ref[:, cols(block, half1)], w1b[block])
+
+    total = sum_over_all(place, sums_of(h1_ref, images), pair_buf.at[0], chip_buf.at[0], sum_sem.at[0], lambda: g2.hop_y(1))
+    mean1, inv1 = norm_of(total, count)
+    scale1 = norm_ref[0:1] * inv1
+    move1 = norm_ref[1:2] - mean1 * scale1
+    g2.hop_core(0)
+    g2.hop_core(1)
+
+    def act1(pixel, row, carry):
+        v = h1_ref[pl.ds(row, images), :] * scale1 + move1
+        put_padded(pad_ref, pixel, (v * sigmoid(v)).astype(BF), images)
+        return carry
+
+    over_pixels(act1, 0, images)
+    g2.hop_y(2)
+    build_patches(pad_ref, patches)
+    if half2 % 128:
+        g2.hop_core(2)
+        gh.hop_y(0)
+        gh.hop_core(0)
+        for piece in range(3):
+            g2.finish(piece)
+        for block in range(n_rep):
+            part = nn(patches[:, block * half2 : (block + 1) * half2], w2b[block])
+            h2_ref[...] = part if block == 0 else h2_ref[...] + part
+    else:
+        h2_ref[...] = nn(patches[:, cols(rep, half2)], w2b[rep])
+        g2.hop_core(2)
+        gh.hop_y(0)
+        gh.hop_core(0)
+        for piece in range(3):
+            g2.finish(piece)
+        for block in g2.blocks():
+            h2_ref[...] += nn(patches[:, cols(block, half2)], w2b[block])
+
+    total = sum_over_all(place, sums_of(h2_ref, images), pair_buf.at[1], chip_buf.at[1], sum_sem.at[1])
+    mean2, inv2 = norm_of(total, count)
+    scale2 = norm_ref[2:3] * inv2
+    move2 = norm_ref[3:4] - mean2 * scale2
+
+    def pool(pixel, row, carry):
+        v = h2_ref[pl.ds(row, images), :] * scale2 + move2
+        return carry + v * sigmoid(v)
+
+    pooled = (over_pixels(pool, jnp.zeros((images, mid), F32), images) / (SIDE * SIDE)).astype(BF)
+    pooled_ref[...] = pooled
+    gh.finish(0)
+    logits = bias_pad[...]
+    for block in range(n_rep):
+        logits = logits + nt(pooled_ref[:, block * head_cols : (block + 1) * head_cols], head_b[block])
+    column = lax.broadcasted_iota(jnp.int32, (images, wide), 1)
+    shown = jnp.where(column < classes, logits, -jnp.inf)
+    top = jnp.max(shown, axis=1, keepdims=True)
+    lse = top + jnp.log(jnp.sum(jnp.exp(shown - top), axis=1, keepdims=True))
+    hit = (column == label_ref[...]).astype(F32)
+    target = jnp.sum(logits * hit, axis=1, keepdims=True)
+    loss_ref[...] = jnp.sum(lse - target, axis=0, keepdims=True)
+    grad = (jnp.exp(shown - lse) - hit) / all_images
+    gbias_ref[...] = jnp.sum(grad, axis=0, keepdims=True)
+    dz = grad.astype(BF)
+    dz_ref[...] = dz
+    for block in range(n_rep):
+        dpool_ref[:, block * head_cols : (block + 1) * head_cols] = nn(dz, head_b[block]) / (SIDE * SIDE)
+    dpool = dpool_ref[...]
+
+    def back2(pixel, row, carry):
+        h = h2_ref[pl.ds(row, images), :]
+        v = h * scale2 + move2
+        sig = sigmoid(v)
+        dy = dpool * sig * (1.0 + v * (1.0 - sig))
+        return carry[0] + dy, carry[1] + dy * ((h - mean2) * inv2)
+
+    zero = jnp.zeros((images, mid), F32)
+    one, two = over_pixels(back2, (zero, zero), images)
+    sums = jnp.concatenate([fold(one), fold(two)], axis=0)
+    total = sum_over_all(place, sums, pair_buf.at[2], chip_buf.at[2], sum_sem.at[2])
+    stat_ref[...] = jnp.concatenate([mean1, inv1, mean2, inv2, total, total], axis=0)
+    for gather in (g1, g2, gh):
+        gather.drain()
+
+
+def run_a(n_dp, n_rep, x, conv1, conv2, head, live1, live2, bias, norm, labels):
+    rows, mid = x.shape[0], conv1.shape[1]
+    images = rows // (SIDE * SIDE)
+    half1, half2 = conv1.shape[0], conv2.shape[0]
+    classes, head_cols = head.shape
+    wide = (classes + 127) // 128 * 128
+    chips = n_dp // 2 * n_rep
+    shape = jax.ShapeDtypeStruct
+    vmem, hbm = pl.BlockSpec(memory_space=pltpu.VMEM), pl.BlockSpec(memory_space=pl.ANY)
+    return pl.pallas_call(
+        functools.partial(kernel_a, n_dp, n_rep),
+        out_shape=(
+            shape((rows, mid), F32), shape((rows, mid), F32),
+            shape((SIDE + 2, (SIDE + 2) * images, mid), BF), shape((n_rep, half2, mid), BF),
+            shape((8, mid), F32), shape((images, wide), BF), shape((images, mid), BF),
+            shape((1, 1), F32), shape((1, wide), F32), shape((images, mid), F32),
+        ),
+        in_specs=[hbm] * 6 + [vmem] * 3,
+        out_specs=[vmem] * 10,
+        scratch_shapes=[
+            pltpu.VMEM(x.shape, BF),
+            pltpu.VMEM((half1, mid), F32), pltpu.VMEM((half1, mid), jnp.int32),
+            pltpu.VMEM((half2, mid), F32), pltpu.VMEM((half2, mid), jnp.int32),
+            pltpu.VMEM((classes, head_cols), F32),
+            pltpu.VMEM((n_rep, half1, mid), BF), pltpu.VMEM((n_rep, wide, head_cols), BF),
+            pltpu.VMEM((rows, 9 * mid), BF), pltpu.VMEM((1, wide), F32),
+            pltpu.VMEM((3, 2, 2, mid), F32), pltpu.VMEM((3, chips, 2, mid), F32),
+            DMA((6,)), DMA((4, 2, 2)), DMA((4, 3, 2)), DMA((4, 1, 2)), DMA((3, 4)),
+        ],
+        compiler_params=pltpu.CompilerParams(
+            collective_id=1, has_side_effects=True, vmem_limit_bytes=60 * 2**20
+        ),
+        name="forward",
+    )(x, conv1, conv2, head, live1, live2, bias, norm, labels)
 
 
 HIGH = lax.Precision.HIGHEST
@@ -34,6 +403,15 @@
     return padded[:, 1 : SIDE + 1, 1 : SIDE + 1, :].reshape(count * SIDE * SIDE, chans)
 
 
+def fold_rows(grad_rows, count, chans):
+    pieces = grad_rows.reshape(SIDE, SIDE, count, 9, chans)
+    padded = jnp.zeros((SIDE + 2, SIDE + 2, count, chans), jnp.float32)
+    for dy in range(3):
+        for dx in range(3):
+            padded = padded.at[dy : dy + SIDE, dx : dx + SIDE].add(pieces[:, :, :, 3 * dy + dx])
+    return padded[1 : SIDE + 1, 1 : SIDE + 1].reshape(count * SIDE * SIDE, chans)
+
+
 def across_rows(left, right):
     return lax.dot_general(
         left, right, (((0,), (0,)), ((), ())), preferred_element_type=jnp.float32
@@ -44,16 +422,6 @@
     return lax.dot_general(
         left, right, (((1,), (1,)), ((), ())), preferred_element_type=jnp.float32
     )
-
-
-def batchnorm_forward(hidden, norm_gain, norm_shift, element_count):
-    sums, squares = lax.psum(
-        (jnp.sum(hidden, axis=0), jnp.sum(hidden * hidden, axis=0)), ("dp", "rep")
-    )
-    channel_mean = sums / element_count
-    inverse_deviation = lax.rsqrt(squares / element_count - channel_mean * channel_mean + NORM_EPS)
-    standardized = (hidden - channel_mean) * inverse_deviation
-    return (norm_gain * standardized + norm_shift, standardized, inverse_deviation)
 
 
 def batchnorm_backward(
@@ -81,22 +449,18 @@
     return lax.dot_general(x, x, (((0,), (0,)), ((), ())), precision=HIGH)
 
 
-def newton_schulz(pair, summed):
-    first, second = pair
+def orthogonal(x, gram):
+    scale = jnp.sqrt(jnp.trace(gram)) + 1e-07
+    gram = gram / (scale * scale)
+    unit = jnp.eye(gram.shape[0], dtype=jnp.float32)
+    product = None
     for turn in range(TURNS):
-        gram_one, gram_two = summed(first, second)
-        if turn == 0:
-            scale_one = jnp.sqrt(jnp.trace(gram_one)) + 1e-07
-            scale_two = jnp.sqrt(jnp.trace(gram_two)) + 1e-07
-            first = first / scale_one
-            second = second / scale_two
-            gram_one = gram_one / (scale_one * scale_one)
-            gram_two = gram_two / (scale_two * scale_two)
-        inner_one = COEF_B * gram_one + COEF_C * jnp.dot(gram_one, gram_one, precision=HIGH)
-        inner_two = COEF_B * gram_two + COEF_C * jnp.dot(gram_two, gram_two, precision=HIGH)
-        first = COEF_A * first + jnp.dot(first, inner_one, precision=HIGH)
-        second = COEF_A * second + jnp.dot(second, inner_two, precision=HIGH)
-    return (first, second)
+        square = jnp.dot(gram, gram, precision=HIGH)
+        factor = COEF_A * unit + COEF_B * gram + COEF_C * square
+        product = factor if product is None else jnp.dot(product, factor, precision=HIGH)
+        if turn < TURNS - 1:
+            gram = jnp.dot(jnp.dot(gram, factor, precision=HIGH), factor, precision=HIGH)
+    return jnp.dot(x / scale, product, precision=HIGH)
 
 
 def adam_update(weight, first, second, grad, rate):
@@ -134,42 +498,24 @@
     classes = class_bias.shape[0]
     all_images = count * lax.axis_size("dp") * lax.axis_size("rep")
     element_count = all_images * SIDE * SIDE
-    part_one = (conv1 * conv1_live.astype(jnp.float32)).astype(jnp.bfloat16)
-    part_two = (conv2 * conv2_live.astype(jnp.float32)).astype(jnp.bfloat16)
-    part_head = classifier.astype(jnp.bfloat16)
-    w1b, w2b, wcb = (
-        lax.all_gather(part_one, "rep", axis=0, tiled=True),
-        lax.all_gather(part_two, "rep", axis=0, tiled=True),
-        lax.all_gather(part_head, "rep", axis=0, tiled=True),
-    )
-    inputs = images.reshape(count * SIDE * SIDE, c_in)
-    hidden_first = jnp.dot(inputs, w1b, preferred_element_type=jnp.float32)
-    normed_first, standardized_first, inverse_deviation_first = batchnorm_forward(
-        hidden_first, batchnorm_parameters[0, 0], batchnorm_parameters[0, 1], element_count
-    )
-    a1 = jax.nn.silu(normed_first).astype(jnp.bfloat16)
-    patches = patches_of(a1.reshape(count, SIDE, SIDE, c_mid))
-    hidden_second = jnp.dot(patches, w2b, preferred_element_type=jnp.float32)
-    normed_second, standardized_second, inverse_deviation_second = batchnorm_forward(
-        hidden_second, batchnorm_parameters[1, 0], batchnorm_parameters[1, 1], element_count
-    )
-    a2 = jax.nn.silu(normed_second)
-    pooled = jnp.mean(a2.reshape(count, SIDE * SIDE, c_mid), axis=1).astype(jnp.bfloat16)
-    logits = jnp.dot(pooled, wcb, preferred_element_type=jnp.float32) + class_bias
-    lse = jax.nn.logsumexp(logits, axis=1)
-    onehot = (labels[:, None] == jnp.arange(classes, dtype=jnp.int32)[None, :]).astype(jnp.float32)
-    target = jnp.sum(logits * onehot, axis=1)
-    probs = jnp.exp(logits - lse[:, None])
-    grad_logits = (probs - onehot) / all_images
-    loss_sum, g_bias = lax.psum(
-        (jnp.sum(lse - target), jnp.sum(grad_logits, axis=0)), ("dp", "rep")
-    )
-    grad_z = grad_logits.astype(jnp.bfloat16)
-    g_class = across_rows(pooled, grad_z)
-    grad_pooled = against_cols(grad_z, wcb) / (SIDE * SIDE)
-    gradient_activation_second = jnp.broadcast_to(
-        grad_pooled[:, None, :], (count, SIDE * SIDE, c_mid)
-    ).reshape(-1, c_mid)
+    n_dp, n_rep = lax.axis_size("dp"), lax.axis_size("rep")
+    x = images.transpose(1, 2, 0, 3).reshape(SIDE * SIDE * count, c_in)
+    (hidden_first, hidden_second, pad, w2b, stat, grad_z, pooled, loss_part, gbias_part, dpool) = run_a(
+        n_dp, n_rep, x, conv1, conv2, classifier.T, conv1_live, conv2_live, class_bias.reshape(1, -1),
+        batchnorm_parameters.reshape(4, c_mid), labels.reshape(-1, 1))
+    w2b = w2b.reshape(-1, c_mid)
+    loss_sum, g_bias = lax.psum((loss_part[0, 0], gbias_part[0, :classes]), ("dp", "rep"))
+    standardized_first = (hidden_first - stat[0]) * stat[1]
+    inverse_deviation_first = stat[1]
+    normed_first = batchnorm_parameters[0, 0] * standardized_first + batchnorm_parameters[0, 1]
+    standardized_second = (hidden_second - stat[2]) * stat[3]
+    inverse_deviation_second = stat[3]
+    normed_second = batchnorm_parameters[1, 0] * standardized_second + batchnorm_parameters[1, 1]
+    inputs = x
+    g_class = across_rows(pooled, grad_z[:, :classes])
+    pieces = [pad[dy:dy+7, dx*count:dx*count+7*count, :].reshape(-1, c_mid) for dy in range(3) for dx in range(3)]
+    patches = jnp.concatenate(pieces, axis=1)
+    gradient_activation_second = jnp.broadcast_to(dpool[None], (49, count, c_mid)).reshape(-1, c_mid)
     grad_h2, gain_two, shift_two = batchnorm_backward(
         gradient_activation_second,
         normed_second,
@@ -180,7 +526,7 @@
     )
     grad_h2 = grad_h2.astype(jnp.bfloat16)
     g_conv2 = across_rows(patches, grad_h2)
-    gradient_activation_first = fold_patches(against_cols(grad_h2, w2b), count, c_mid)
+    gradient_activation_first = fold_rows(against_cols(grad_h2, w2b), count, c_mid)
     grad_h1, gain_one, shift_one = batchnorm_backward(
         gradient_activation_first,
         normed_first,
@@ -199,10 +545,8 @@
     mom_one = 0.5 * conv1_mom + rows_one
     mom_two = 0.5 * conv2_mom + rows_two
 
-    def summed(first, second):
-        return lax.psum((gram_of(first), gram_of(second)), "rep")
-
-    ortho_one, ortho_two = newton_schulz((mom_one, mom_two), summed)
+    gram_one, gram_two = lax.psum((gram_of(mom_one), gram_of(mom_two)), "rep")
+    ortho_one, ortho_two = orthogonal(mom_one, gram_one), orthogonal(mom_two, gram_two)
     conv1_new = (conv1 - 1.0 * ortho_one) * conv1_next.astype(jnp.float32)
     conv2_new = (conv2 - 1.0 * ortho_two) * conv2_next.astype(jnp.float32)
     head_new, head_m, head_v = adam_update(classifier, class_m, class_v, rows_head, 0.03)

time: 1240 us -> 699 us (0.56)
  waiting for transfers between devices: 622 us -> 373 us
  local copies, waits for them, and re-layouts: 142 us -> 18.7 us
  blocking collectives: 189 us -> 79.4 us
  matrix products: 220 us -> 120 us
  Pallas kernels: 0 us -> 62.1 us
  other arithmetic: 45.3 us -> 23.4 us
    psum x5 -> x1, waiting for transfers between devices: 302 us -> 54.3 us  [local(): gram_one, gram_two = lax.psum((gram_of(mom_one), gram_of(mom_two)), 'rep')]
    psum x3 -> x1, blocking collectives: 123 us -> 40.3 us  [local(): lax.psum((loss_part[0, 0], gbias_part[0, :classes]), ('dp', 'rep'))]
    pallas_call x0 -> x1, Pallas kernels: none -> 62.1 us  [run_a(): pl.pallas_call(functools.partial(kernel_a, n_dp, n_rep), out_shape=(shape...]
    dot_general x10 -> x2, matrix products: 66.7 us -> 13.5 us  [gram_of(): return lax.dot_general(x, x, (((0,), (0,)), ((), ())), precision=HIGH)]
    slice x5 -> x2, local copies, waits for them, and re-layouts: 52.8 us -> 1.11 us  [the longest x1 0.9 us: local(): pad[dy:dy + 7, dx * count:dx * count + 7 * count, :].reshape(-1, c_mid)]
    dot_general x23 -> x36, matrix products: 124 us -> 83.6 us  [the longest x10 22.3 us: orthogonal(): square = jnp.dot(gram, gram, precision=HIGH)]
    reshape x6 -> x2, local copies, waits for them, and re-layouts: 30.8 us -> 2.64 us  [the longest x1 1.33 us: local(): labels.reshape(-1, 1)]
    all_gather x1 -> x0, blocking collectives: 26.8 us -> none  [local(): lax.all_gather(part_head, 'rep', axis=0, tiled=True)]
  transfers between devices with their start and end apart: 11 -> 5, of which waited for: 9 -> 4; matrix products, arithmetic and copies ran while one was open for 9% -> 7% of each run, Pallas kernels for 0% -> 0%
where the time goes in v1:
time: 699 us; the launch traced here: 693 us
  waiting for transfers between devices  373 us (53%)
  matrix products  120 us (17%)
  blocking collectives  79.4 us (11%)
  Pallas kernels  62.1 us (9%)
  other arithmetic  23.4 us (3%)
  local copies, waits for them, and re-layouts  18.7 us (3%)
  between operations  16.2 us (2%)
    psum x1, waiting for transfers between devices, local(): lax.psum((rows_one, rows_two, rows_head), 'dp')  163 us
    reduce_scatter x1, waiting for transfers between devices, local(): lax.psum_scatter(g_conv2, 'rep', scatter_dimension=0, tiled=True)  113 us
    pallas_call x1, Pallas kernels, run_a(): pl.pallas_call(functools.partial(kernel_a, n_dp, n_rep), out_shape=(shape...  62.1 us
    psum x1, waiting for transfers between devices, local(): gram_one, gram_two = lax.psum((gram_of(mom_one), gram_of(mom_two)), 'rep')  54.3 us
    reduce_scatter x1, waiting for transfers between devices, local(): lax.psum_scatter(g_conv1, 'rep', scatter_dimension=0, tiled=True)  43 us
    psum x1, blocking collectives, local(): lax.psum((loss_part[0, 0], gbias_part[0, :classes]), ('dp', 'rep'))  40.3 us
    psum x1, blocking collectives, batchnorm_backward(): lax.psum((jnp.sum(normed_gradient, axis=0), jnp.sum(normed_gradient * sta...  39.1 us
    dot_general x10, matrix products, orthogonal(): square = jnp.dot(gram, gram, precision=HIGH)  22.3 us
  transfers between devices with their start and end apart: 5, of which 4 were waited for; matrix products, arithmetic and copies ran while one was open for 7% of the time, Pallas kernels for 0%

profile of v1, /device:TPU:0, one launch (start us, length us, event | category | flops | bytes accessed | tf_op | source)
XLA Modules:
  0.0 693.5 jit_solution(3971907072451938165)
XLA Ops:
  7.2 1.3 reshape.470.refs_7_
  8.5 1.3 copy.34.refs_8_
  9.9 62.1 %forward.1 = (f32[784,512]{1,0:T(8,128)}, f32[784,512]{1,0:T(8,128)}, bf16[9,144,512]{2,1,0:T(8,128)(2,1)}, bf16[2,2304,512]{2,1,0:T(8,128)(2,1)}, f32[8,512]{1,...) custom-call(bf16[784,2048]{1,0:T(8,128)(2,1)} %bitcast.215, ...), custom_call_target="tpu_custom_call" | custom-call | tf_op jit(solution)/shard_map/forward/pallas_call | solution.py:353
  72.0 2.7 fusion.44
  75.7 39.1 %all-reduce.2 = (f32[512]{0:T(512)S(1)}, f32[512]{0:T(512)S(1)}) all-reduce(f32[512]{0:T(512)S(1)} %get-tuple-element.159, f32[512]{0:T(512)S(1)} %get-tuple-element.158), channel_id=1, replica_groups=mesh['dp'=16,'rep'=2] {'dp','rep'}, use_global_device_ids=true, to_apply=%region_4.0 | all-reduce | flops 1024 | bytes 8192 | tf_op jit(solution)/shard_map/psum | solution.py:432
  115.8 6.3 fusion.59
  124.8 1.7 fusion.19
  126.5 2.4 fusion.5
  131.7 1.2 copy-done.5
  132.9 2.0 fusion.50
  134.9 40.3 %all-reduce.1 = (f32[]{:T(128)}, f32[512]{0:T(512)S(1)}, f32[512]{0:T(512)S(1)}, f32[1000]{0:T(1024)S(1)}) all-reduce(f32[]{:T(128)} %bitcast.5, f32[512]{0:T(512)S(1)} %get-tuple-element.161, f32[512]{0:T(512)S(1)} %get-tuple-element.160, f32[1000]{0:T(1024)S(1)} %bitcast.253), channel_id=1, replica_groups=mesh['dp'=16,'rep'=2] {'dp','rep'}, use_global_device_ids=true, to_apply=%region_0.0 | all-reduce | flops 2025 | bytes 16200 | tf_op jit(solution)/shard_map/psum | solution.py:507
  175.2 6.4 convolution_bitcast_fusion
  181.7 1.2 copy-done.1
  185.3 7.6 %fusion.72 = f32[4608,512]{1,0:T(8,128)} fusion(bf16[784,4608]{1,0:T(8,128)(2,1)S(1)} %constant_dynamic-update-slice_fusion, bf16[784,512]{1,0:T(8,128)(2,1)S(1)} %copy-done.15), kind=kOutput, calls=%fused_computation.143 | convolution fusion | flops 3699376128 | bytes 17465344 | tf_op jit(solution)/shard_map/dot_general | solution.py:416
  193.0 43.0 %reduce-scatter.4.cloned.1.call-done = f32[1024,512]{0,1:T(8,128)} async-done(((f32[2048,512]{0,1:T(8,128)}), f32[1024,512]{0,1:T(8,128)}) %reduce-scatter.4.cloned.1.call-update) | async-done | bytes 2097168 | tf_op jit(solution)/shard_map/reduce_scatter | solution.py:540
  236.0 113.0 %reduce-scatter.6.cloned.1.call-done = f32[2304,512]{1,0:T(8,128)} async-done(((f32[4608,512]{1,0:T(8,128)}), f32[2304,512]{1,0:T(8,128)}) %reduce-scatter.6.cloned.1.call-update) | async-done | bytes 4718608 | tf_op jit(solution)/shard_map/reduce_scatter | solution.py:541
  349.1 1.5 copy-done.11
  350.6 2.2 copy.35
  352.8 163.0 %all-reduce.8.cloned.1.call-done = (f32[1024,512]{0,1:T(8,128)}, f32[2304,512]{1,0:T(8,128)}, f32[256,1000]{0,1:T(8,128)}) async-done(((f32[1024,512]{0,1:T(8,128)}, f32[2304,512]{1,0:T(8,128)}, f32[256,1000]{0,1:T(8,128)}), (f32[1024,512]{0,1:T(8,128)}, f32[2304,512]{1,0:T(8,128)}, f32[256,1000]{0,1:T(8,128)})) %all-reduce.8.cloned.1.call-update) | async-done | bytes 7839760 | tf_op jit(solution)/shard_map/psum | solution.py:544
  515.8 2.8 multiply_add_fusion.1
  518.6 4.5 fusion.60
  523.1 1.2 multiply_add_fusion
  524.3 2.2 copy-done
  526.5 9.0 %fusion.73 = f32[512,512]{1,0:T(8,128)} fusion(f32[2304,512]{1,0:T(8,128)S(1)} %multiply_add_fusion), kind=kOutput, calls=%fused_computation.144 | convolution fusion | flops 7247757312 | bytes 5767168 | tf_op jit(solution)/shard_map/dot_general | solution.py:449
  538.1 1.8 copy.44
  540.0 4.6 multiply_subtract_fusion
  544.5 54.3 %all-reduce.10.cloned.1.call-done = (f32[512,512]{1,0:T(8,128)}, f32[512,512]{1,0:T(8,128)}) async-done(((f32[512,512]{1,0:T(8,128)}, f32[512,512]{1,0:T(8,128)}), (f32[512,512]{1,0:T(8,128)}, f32[512,512]{1,0:T(8,128)})) %all-reduce.10.cloned.1.call-update) | async-done | bytes 2097168 | tf_op jit(solution)/shard_map/psum | solution.py:548
  598.8 2.4 select_reduce_fusion
  601.9 1.9 fusion.33
  603.8 1.9 fusion.42
  605.7 1.8 fusion.61
  607.6 1.9 fusion.32
  609.5 2.8 fusion.62
  612.3 2.8 fusion.63
  615.9 4.6 fusion.28
  620.4 1.9 fusion.43
  622.3 1.8 fusion.74
  624.2 1.9 fusion.27
  626.1 1.8 fusion.75
  628.0 1.8 fusion.76
  629.8 1.8 fusion.64
  631.7 2.1 fusion.31
  633.8 1.8 fusion.66
  635.7 1.8 fusion.65
  637.5 1.8 fusion.67
  639.4 1.9 fusion.30
  641.3 1.8 fusion.69
  643.1 1.8 fusion.68
  645.0 2.1 fusion.70
  647.1 1.9 fusion.29
  649.0 1.8 fusion.77
  650.8 1.9 fusion.26
  652.7 1.8 fusion.79
  654.6 1.8 fusion.78
  656.4 1.8 fusion.80
  658.3 2.3 fusion.25
  660.6 1.8 fusion.82
  662.5 1.9 fusion.81
  664.4 1.8 fusion.83
  666.2 1.9 fusion.24
  668.2 1.9 fusion.71
  670.1 5.2 convert_multiply_fusion
  675.3 1.8 fusion.84
  677.2 9.6 %fusion = f32[2304,512]{1,0:T(8,128)} fusion(f32[2304,512]{1,0:T(8,128)S(1)} %bitcast.220, f32[512,512]{1,0:T(8,128)S(1)} %fusion.84, s32[2304,512]{1,0:T(8,128)S(1)} %bitcast.256, f32[2304,512]{1,0:T(8,128)S(1)} %bitcast.214, f32[]{:T(128)S(6)} %add.274), kind=kOutput, calls=%fused_computation.1 | convolution fusion | flops 7252475904 | bytes 19922948 | tf_op jit(solution)/shard_map/dot_general | solution.py:463
  (114 shorter events, 12.6 us)
Async XLA Ops:
  7.2 185.8 %reduce-scatter.8.cloned.1.call-start = ((), (), s32[]{:S(2)}) async-start(), calls=%async_computation.5 | async-start | bytes 3072000 | tf_op jit(solution)/shard_map/reduce_scatter | solution.py:542
  71.9 2.8 copy-start.17
  72.0 2.8 copy-start.21
  72.0 2.8 copy-start.4
  72.0 2.8 copy-start.16
  74.7 161.3 %reduce-scatter.4.cloned.1.call-start = ((), (), s32[]{:S(2)}) async-start(), calls=%async_computation.3 | async-start | bytes 6291456 | tf_op jit(solution)/shard_map/reduce_scatter | solution.py:540
  115.8 6.3 copy-start.14
  122.8 0.7 copy-start.25
  131.5 1.4 copy-start.5
  132.9 2.0 copy-start.24
  132.9 42.3 %copy-start.2 = (bf16[16,7,7,2048]{3,0,2,1:T(8,128)(2,1)S(1)}, bf16[16,7,7,2048]{3,0,2,1:T(8,128)(2,1)}, u32[]{:S(2)}) copy-start(bf16[16,7,7,2048]{3,0,2,1:T(8,128)(2,1)} %param.37) | copy-start | bytes 9633796
  181.6 1.3 copy-start.1
  181.6 167.4 %reduce-scatter.6.cloned.1.call-start = ((), (), s32[]{:S(2)}) async-start(), calls=%async_computation.4 | async-start | bytes 14155776 | tf_op jit(solution)/shard_map/reduce_scatter | solution.py:541
  184.2 1.1 copy-start.15
  192.9 322.9 %all-reduce.8.cloned.1.call-start = ((), (), s32[]{:S(2)}) async-start(), calls=%async_computation.6 | async-start | bytes 15679488 | tf_op jit(solution)/shard_map/psum | solution.py:544
  349.0 1.6 copy-start.11
  349.0 249.8 %all-reduce.10.cloned.1.call-start = ((), (), s32[]{:S(2)}) async-start(), calls=%async_computation.7 | async-start | bytes 4194304 | tf_op jit(solution)/shard_map/psum | solution.py:548
  515.8 7.3 %slice-start.2 = ((s8[4718592]{0:T(1024)(128)(4,1)}), s8[4194304]{0:T(1024)(128)(4,1)S(1)}, s32[]{:S(2)}) async-start(s8[4718592]{0:T(1024)(128)(4,1)} %bitcast.217), calls=%async_computation.10 | async-start | bytes 8388608
  515.8 7.3 %slice-start.3 = ((s8[4718592]{0:T(1024)(128)(4,1)}), s8[524288]{0:T(1024)(128)(4,1)S(1)}, s32[]{:S(2)}) async-start(s8[4718592]{0:T(1024)(128)(4,1)} %bitcast.217), calls=%async_computation.11 | async-start | bytes 1048576
  518.6 4.5 copy-start.6
  524.3 2.2 copy-start
  535.6 0.7 copy-start.19
  535.6 0.7 copy-start.20
  535.6 2.0 copy-start.18
  535.6 2.0 copy-start.22
  535.6 2.0 copy-start.23
  538.1 1.8 copy-start.9
  598.8 3.1 copy-start.13
  615.8 4.6 copy-start.12
  627.9 1.9 copy-start.8
  633.8 1.9 copy-start.7
  647.1 30.1 %slice-start.6 = ((s8[4718592]{0:T(1024)(128)(4,1)}), s8[4194304]{0:T(1024)(128)(4,1)S(1)}, s32[]{:S(2)}) async-start(s8[4718592]{0:T(1024)(128)(4,1)} %bitcast.255), calls=%async_computation.14 | async-start | bytes 8388608
  662.5 14.7 %slice-start.7 = ((s8[4718592]{0:T(1024)(128)(4,1)}), s8[524288]{0:T(1024)(128)(4,1)S(1)}, s32[]{:S(2)}) async-start(s8[4718592]{0:T(1024)(128)(4,1)} %bitcast.255), calls=%async_computation.15 | async-start | bytes 1048576
  664.3 5.7 copy-start.10
  666.2 3.8 copy-start.3
  666.2 10.9 %slice-start.4 = ((s8[4718592]{0:T(1024)(128)(4,1)}), s8[4194304]{0:T(1024)(128)(4,1)S(1)}, s32[]{:S(2)}) async-start(s8[4718592]{0:T(1024)(128)(4,1)} %bitcast.219), calls=%async_computation.12 | async-start | bytes 8388608
  668.2 9.0 %slice-start = ((s8[4718592]{0:T(1024)(128)(4,1)}), s8[4194304]{0:T(1024)(128)(4,1)S(1)}, s32[]{:S(2)}) async-start(s8[4718592]{0:T(1024)(128)(4,1)} %bitcast.213), calls=%async_computation.8 | async-start | bytes 8388608
  670.1 7.1 %slice-start.1 = ((s8[4718592]{0:T(1024)(128)(4,1)}), s8[524288]{0:T(1024)(128)(4,1)S(1)}, s32[]{:S(2)}) async-start(s8[4718592]{0:T(1024)(128)(4,1)} %bitcast.213), calls=%async_computation.9 | async-start | bytes 1048576
  670.1 7.1 %slice-start.5 = ((s8[4718592]{0:T(1024)(128)(4,1)}), s8[524288]{0:T(1024)(128)(4,1)S(1)}, s32[]{:S(2)}) async-start(s8[4718592]{0:T(1024)(128)(4,1)} %bitcast.219), calls=%async_computation.13 | async-start | bytes 1048576
Sparse Core Ops, SparseCore 0:
  74.8 29.8 reduce-scatter.7
  181.7 54.2 reduce-scatter.3
  238.4 110.5 reduce-scatter.5
  353.3 162.4 all-reduce.7
  535.7 63.0 all-reduce.9
